TPU v7x, 32 devices: a whole 2x2x4 slice. The times are simulated.
32 devices in a mesh: aux: 4 (over y, x), occ: 8 (over z, core).
Axes of the slice: x: 2, y: 2, z: 4, core: 2. Of those that a mesh axis runs over, the one named last changes fastest.
Arguments:
- amplitudes: bfloat16 [32, 512, 1024], P('aux', 'occ'), may hold values from -6 to 6
- virtual_orbitals: bfloat16 [1536, 1024], P('aux'), may hold values from -0.1875 to 0.1875
- occupied_orbitals: bfloat16 [1536, 512], P('aux'), may hold values from -0.25 to 0.25
- screening: int32 [12, 12], replicated, may hold values from 0 to 1, as said below
- pair_owner: int32 [12, 12], replicated, may hold values from 0 to 7, as said below
- pair_weight: bfloat16 [16, 128, 128], P('occ'), may hold values from 0.5 to 2
Outputs:
- owned_density: bfloat16 [32, 16, 128, 128], P('aux', 'occ')
Inputs may be any that keep to these rules, and one draw needn't show every extreme that they name: `screening`: Symmetric; exactly 9 blocks (r, c) with r <= c are 1. `pair_owner`: Symmetric. Among kept blocks with r <= c, no owner holds more than 2, and some owner holds exactly 2.
All inputs are finite; a program needn't handle non-finite values.
Results may differ from a plain program's by a relative error of at most 0.0085.
Values may be sent and summed in bfloat16 or wider, within the bound.
A program may use at most 64 MiB of HBM per device.

v0:
```python
import jax
import jax.numpy as jnp
from jax import lax
from jax.sharding import PartitionSpec as P

MAXP = 2


def slot_table(screening, pair_owner, slots):
    nblocks = screening.shape[0]
    count = nblocks * nblocks
    block_ids = jnp.arange(count, dtype=jnp.int32)
    first = block_ids // nblocks
    second = block_ids % nblocks
    keep_flag = (screening.reshape(count) == 1) & (first <= second)
    owner_flat = pair_owner.reshape(count)
    earlier = (
        (owner_flat[:, None] == owner_flat[None, :])
        & keep_flag[None, :]
        & (block_ids[None, :] < block_ids[:, None])
    )
    ranks = jnp.sum(earlier.astype(jnp.int32), axis=1)
    target = jnp.where(keep_flag, owner_flat * MAXP + ranks, -1)
    matches = target[None, :] == jnp.arange(slots, dtype=jnp.int32)[:, None]
    filled = jnp.any(matches, axis=1)
    chosen = jnp.sum(jnp.where(matches, block_ids[None, :], 0), axis=1)
    return (filled, chosen // nblocks, chosen % nblocks)


def per_device(amplitudes, virtual_orbitals, occupied_orbitals, screening, pair_owner, pair_weight):
    group_size, occupied_local, virtual_count = amplitudes.shape
    moved = lax.all_to_all(amplitudes, "occ", split_axis=0, concat_axis=1, tiled=True)
    own_functions, occupied_all, _ = moved.shape
    flat_moved = moved.reshape(own_functions * occupied_all, virtual_count)
    product = lax.dot_general(
        flat_moved,
        lax.all_gather(virtual_orbitals, "aux", axis=0, tiled=True),
        (((1,), (1,)), ((), ())),
        preferred_element_type=jnp.float32,
    )
    half_moved = product.astype(jnp.bfloat16)
    regrouped = half_moved.reshape(own_functions, occupied_all, half_moved.shape[1])
    product = jnp.einsum(
        "mi,pin->pmn",
        lax.all_gather(occupied_orbitals, "aux", axis=0, tiled=True),
        regrouped,
        preferred_element_type=jnp.float32,
    )
    full = product.astype(jnp.bfloat16)
    own_count = full.shape[0]
    nblocks = screening.shape[0]
    width = full.shape[1] // nblocks
    slots = lax.axis_size("occ") * MAXP
    filled, row_blocks, col_blocks = slot_table(screening, pair_owner, slots)
    grid = full.reshape(own_count, nblocks, width, nblocks, width)
    members = jnp.arange(own_count, dtype=jnp.int32)[:, None]
    direct = grid[members, row_blocks[None, :], :, col_blocks[None, :], :]
    mirror = grid[members, col_blocks[None, :], :, row_blocks[None, :], :]
    present = filled[None, :, None, None]
    direct = jnp.where(present, direct, jnp.zeros_like(direct))
    mirror = jnp.where(present, mirror, jnp.zeros_like(mirror))
    local_fold = (
        direct.astype(jnp.float32) + jnp.swapaxes(mirror, -1, -2).astype(jnp.float32)
    ).astype(jnp.bfloat16)
    folded = lax.all_to_all(local_fold, "occ", split_axis=1, concat_axis=0, tiled=True)
    weights = pair_weight.astype(jnp.float32)[None]
    return (weights * folded.astype(jnp.float32)).astype(jnp.bfloat16)


def solution(mesh):
    return jax.shard_map(
        per_device,
        mesh=mesh,
        in_specs=(
            P("aux", "occ", None),
            P("aux", None),
            P("aux", None),
            P(),
            P(),
            P("occ", None, None),
        ),
        out_specs=P("aux", "occ", None, None),
        check_vma=False,
    )
```

profile of v0, /device:TPU:0, one launch (start us, length us, event | category | flops | bytes accessed | tf_op | source)
XLA Modules:
  0.0 151.5 jit_solution(8574477358672630655)
XLA Ops:
  6.5 0.0 copy-start.2
  6.5 0.0 copy-start.1
  6.5 0.0 all-gather.5.cloned.1.call-start
  6.5 0.7 all-gather.5.cloned.1.call-update
  7.3 0.0 all-gather.3.cloned.1.call-start
  7.3 0.7 all-gather.3.cloned.1.call-update
  8.0 6.3 %all-to-all-start = ((bf16[8,64,1024]{2,1,0:T(8,128)(2,1)}), bf16[8,64,1024]{2,1,0:T(8,128)(2,1)S(1)}, u32[]{:S(2)}, u32[]{:S(2)}) async-start(bf16[8,64,1024]{2,1,0:T(8,128)(2,1)} %param.6), calls=%async_computation | async-start | bytes 2097152 | tf_op jit(solution)/shard_map/all_to_all | solution.py:32
  14.3 0.0 copy-done.2
  14.4 0.1 reshape.167
  14.4 0.0 copy-done.1
  14.5 0.1 eq.50
  14.6 0.2 convert_reduce_fusion
  14.8 0.1 select_reduce_fusion
  15.0 0.1 fusion.5
  15.1 25.9 %all-to-all-done = bf16[8,64,1024]{2,1,0:T(8,128)(2,1)S(1)} async-done(((bf16[8,64,1024]{2,1,0:T(8,128)(2,1)}), bf16[8,64,1024]{2,1,0:T(8,128)(2,1)S(1)}, u32[]{:S(2)}, u32[]{:S(2)}) %all-to-all-start) | async-done | bytes 1048608 | tf_op jit(solution)/shard_map/all_to_all | solution.py:32
  40.9 2.0 %all-gather.5.cloned.1.call-done = bf16[1536,512]{1,0:T(8,128)(2,1)} async-done(((bf16[384,512]{1,0:T(8,128)(2,1)}), bf16[1536,512]{1,0:T(8,128)(2,1)}) %all-gather.5.cloned.1.call-update) | async-done | bytes 1572880 | tf_op jit(solution)/shard_map/all_gather | solution.py:45
  42.9 45.8 %all-gather.3.cloned.1.call-done = bf16[1536,1024]{1,0:T(8,128)(2,1)} async-done(((bf16[384,1024]{1,0:T(8,128)(2,1)}), bf16[1536,1024]{1,0:T(8,128)(2,1)}) %all-gather.3.cloned.1.call-update) | async-done | bytes 3145744 | tf_op jit(solution)/shard_map/all_gather | solution.py:37
  88.8 9.4 %fusion = bf16[1,1536,1536]{1,2,0:T(8,128)(2,1)} fusion(bf16[1536,512]{1,0:T(8,128)(2,1)} %all-gather.5.cloned.1.call-done, bf16[512,1024]{1,0:T(8,128)(2,1)S(1)} %bitcast.52, bf16[1536,1024]{1,0:T(8,128)(2,1)} %all-gather.3.cloned.1.call-done), kind=kOutput, calls=%fused_computation.3 | convolution fusion | flops 4029677568 | bytes 10485760 | tf_op jit(solution)/shard_map/mi,pin->pmn/dot_general | solution.py:43
  98.1 9.4 %reshape.187 = bf16[1,12,128,12,128]{2,1,4,3,0:T(8,128)(2,1)} reshape(bf16[1,1536,1536]{1,2,0:T(8,128)(2,1)} %fusion) | data formatting | bytes 9437184 | tf_op jit(solution)/shard_map/reshape | solution.py:55
  107.5 8.8 %copy.24 = bf16[1,12,128,12,128]{4,2,3,1,0:T(8,128)(2,1)} copy(bf16[1,12,128,12,128]{2,1,4,3,0:T(8,128)(2,1)} %reshape.187) | data formatting | bytes 9437184 | tf_op jit(solution)/shard_map/reshape | solution.py:55
  116.3 0.0 copy-start
  116.3 3.0 %gather_fusion.1 = bf16[16,128,128]{2,1,0:T(8,128)(2,1)S(1)} fusion(bf16[1,12,128,12,128]{4,2,3,1,0:T(8,128)(2,1)} %copy.24, s32[16]{0:T(128)S(1)} %get-tuple-element.9), kind=kCustom, calls=%fused_computation.1 | custom fusion | bytes 1048768 | tf_op jit(solution)/shard_map/gather | solution.py:58
  119.4 0.3 copy.28
  119.6 3.0 %gather_fusion = bf16[16,128,128]{2,1,0:T(8,128)(2,1)S(1)} fusion(bf16[1,12,128,12,128]{4,2,3,1,0:T(8,128)(2,1)} %copy.24, s32[16]{0:T(128)S(1)} %get-tuple-element.10), kind=kCustom, calls=%fused_computation | custom fusion | bytes 1048768 | tf_op jit(solution)/shard_map/gather | solution.py:57
  122.6 1.1 fusion.3
  123.7 4.6 %all-to-all-start.1 = ((bf16[1,16,128,128]{3,2,0,1:T(8,128)(2,1)}), bf16[1,16,128,128]{3,2,0,1:T(8,128)(2,1)S(1)}, u32[]{:S(2)}, u32[]{:S(2)}) async-start(bf16[1,16,128,128]{3,2,0,1:T(8,128)(2,1)} %fusion.3), calls=%async_computation.1 | async-start | bytes 1048576 | tf_op jit(solution)/shard_map/all_to_all | solution.py:65
  128.3 0.0 copy-done
  128.3 15.3 %all-to-all-done.1 = bf16[1,16,128,128]{3,2,0,1:T(8,128)(2,1)S(1)} async-done(((bf16[1,16,128,128]{3,2,0,1:T(8,128)(2,1)}), bf16[1,16,128,128]{3,2,0,1:T(8,128)(2,1)S(1)}, u32[]{:S(2)}, u32[]{:S(2)}) %all-to-all-start.1) | async-done | bytes 524320 | tf_op jit(solution)/shard_map/all_to_all | solution.py:65
  143.7 0.9 fusion.1
  (8 shorter events, 0.1 us)
Async XLA Ops:
  6.5 7.8 %copy-start.2 = (s32[12,12]{1,0:T(8,128)S(1)}, s32[12,12]{1,0:T(8,128)}, u32[]{:S(2)}) copy-start(s32[12,12]{1,0:T(8,128)} %param.10) | copy-start | bytes 1732
  6.5 7.9 %copy-start.1 = (s32[12,12]{1,0:T(8,128)S(1)}, s32[12,12]{1,0:T(8,128)}, u32[]{:S(2)}) copy-start(s32[12,12]{1,0:T(8,128)} %param.9) | copy-start | bytes 1732
  6.5 36.4 %all-gather.5.cloned.1.call-start = ((), (), s32[]{:S(2)}) async-start(), calls=%async_computation.3 | async-start | bytes 1966080 | tf_op jit(solution)/shard_map/all_gather | solution.py:45
  7.3 81.5 %all-gather.3.cloned.1.call-start = ((), (), s32[]{:S(2)}) async-start(), calls=%async_computation.2 | async-start | bytes 3932160 | tf_op jit(solution)/shard_map/all_gather | solution.py:37
  8.0 32.9 %all-to-all-start = ((bf16[8,64,1024]{2,1,0:T(8,128)(2,1)}), bf16[8,64,1024]{2,1,0:T(8,128)(2,1)S(1)}, u32[]{:S(2)}, u32[]{:S(2)}) async-start(bf16[8,64,1024]{2,1,0:T(8,128)(2,1)} %param.6), calls=%async_computation | async-start | bytes 2097152 | tf_op jit(solution)/shard_map/all_to_all | solution.py:32
  116.3 12.0 %copy-start = (bf16[2,128,128]{2,1,0:T(8,128)(2,1)S(1)}, bf16[2,128,128]{2,1,0:T(8,128)(2,1)}, u32[]{:S(2)}) copy-start(bf16[2,128,128]{2,1,0:T(8,128)(2,1)} %param.11) | copy-start | bytes 196612
  123.7 20.0 %all-to-all-start.1 = ((bf16[1,16,128,128]{3,2,0,1:T(8,128)(2,1)}), bf16[1,16,128,128]{3,2,0,1:T(8,128)(2,1)S(1)}, u32[]{:S(2)}, u32[]{:S(2)}) async-start(bf16[1,16,128,128]{3,2,0,1:T(8,128)(2,1)} %fusion.3), calls=%async_computation.1 | async-start | bytes 1048576 | tf_op jit(solution)/shard_map/all_to_all | solution.py:65
Sparse Core Ops, SparseCore 0:
  9.2 33.6 all-gather.4
  44.7 43.9 all-gather.2
where the time goes:
time: 152 us; the launch traced here: 151 us
  waiting for transfers between devices  90.4 us (59%)
  local copies, waits for them, and re-layouts  24.7 us (16%)
  between operations  13.5 us (9%)
  starting transfers between devices  11 us (7%)
  matrix products  9.37 us (6%)
  other arithmetic  2.53 us (2%)
    all_gather x1, waiting for transfers between devices, per_device(): lax.all_gather(virtual_orbitals, 'aux', axis=0, tiled=True)  45.8 us
    all_to_all x1, waiting for transfers between devices, per_device(): lax.all_to_all(amplitudes, 'occ', split_axis=0, concat_axis=1, tiled=True)  25.9 us
    reshape x2, local copies, waits for them, and re-layouts, per_device(): grid = full.reshape(own_count, nblocks, width, nblocks, width)  18.2 us
    all_to_all x1, waiting for transfers between devices, per_device(): lax.all_to_all(local_fold, 'occ', split_axis=1, concat_axis=0, tiled=True)  15.3 us
    dot_general x1, matrix products, per_device(): jnp.einsum('mi,pin->pmn', lax.all_gather(occupied_orbitals, 'aux', axis=0...  9.37 us
    all_to_all x1, starting transfers between devices, per_device(): lax.all_to_all(amplitudes, 'occ', split_axis=0, concat_axis=1, tiled=True)  6.34 us
    all_to_all x1, starting transfers between devices, per_device(): lax.all_to_all(local_fold, 'occ', split_axis=1, concat_axis=0, tiled=True)  4.6 us
    gather x2, local copies, waits for them, and re-layouts, per_device(): mirror = grid[members, col_blocks[None, :], :, row_blocks[None, :], :]  3.3 us
  transfers between devices with their start and end apart: 4, of which 4 were waited for; matrix products, arithmetic and copies ran while one was open for 0% of the time, Pallas kernels for 0%

commit v1 on v0

v1 whole, which is shorter than its diff:
```python
import functools

import jax
import jax.numpy as jnp
from jax import lax
from jax.experimental import pallas as pl
from jax.experimental.pallas import tpu as pltpu
from jax.sharding import PartitionSpec as P

MAXP = 2
MESH = pl.DeviceIdType.MESH


def slot_table(screening, pair_owner, slots):
    nblocks = screening.shape[0]
    count = nblocks * nblocks
    block_ids = jnp.arange(count, dtype=jnp.int32)
    first = block_ids // nblocks
    second = block_ids % nblocks
    keep_flag = (screening.reshape(count) == 1) & (first <= second)
    owner_flat = pair_owner.reshape(count)
    earlier = (
        (owner_flat[:, None] == owner_flat[None, :])
        & keep_flag[None, :]
        & (block_ids[None, :] < block_ids[:, None])
    )
    ranks = jnp.sum(earlier.astype(jnp.int32), axis=1)
    target = jnp.where(keep_flag, owner_flat * MAXP + ranks, -1)
    matches = target[None, :] == jnp.arange(slots, dtype=jnp.int32)[:, None]
    filled = jnp.any(matches, axis=1)
    chosen = jnp.sum(jnp.where(matches, block_ids[None, :], 0), axis=1)
    return filled, chosen // nblocks, chosen % nblocks


def fused(
    groups, peers,
    row_blocks, col_blocks, amp, virt, occ, out,
    moved, virt_all, occ_all, half, fold,
    x_send, x_recv, g_send, g_recv, s_send, s_recv, f_send, f_recv, local,
):
    aux = lax.axis_index("aux")
    me = lax.axis_index("occ")
    core = lax.rem(me, 2)
    sibling = me + 1 - 2 * core
    own = moved.shape[1]
    inner = moved.shape[2]
    rows = virt.shape[0]
    part = rows // 2
    width = half.shape[2]
    per_shard = rows // width

    def away(j):
        return lax.rem(me + j, peers)

    def other(j):
        return lax.rem(aux + j, groups)

    barrier = pltpu.get_barrier_semaphore()

    def greet(j, carry):
        pl.semaphore_signal(barrier, inc=1, device_id={"occ": away(j)}, device_id_type=MESH)
        return carry

    lax.fori_loop(1, peers, greet, 0)
    for j in range(1, groups):
        pl.semaphore_signal(barrier, inc=1, device_id={"aux": other(j)}, device_id_type=MESH)

    keep = [
        pltpu.make_async_copy(virt, virt_all.at[pl.ds(pl.multiple_of(aux * rows, rows), rows)], local.at[0]),
        pltpu.make_async_copy(occ, occ_all.at[pl.ds(aux * per_shard, per_shard)], local.at[1]),
        pltpu.make_async_copy(amp.at[pl.ds(me * own, own)], moved.at[me], local.at[2]),
    ]
    for copy in keep:
        copy.start()
    pl.semaphore_wait(barrier, peers - 1 + groups - 1)

    def x_copy(j):
        to = away(j)
        return pltpu.make_async_remote_copy(
            src_ref=amp.at[pl.ds(to * own, own)],
            dst_ref=moved.at[me],
            send_sem=x_send.at[j - 1],
            recv_sem=x_recv.at[j - 1],
            device_id={"occ": to},
            device_id_type=MESH,
        )

    def halves(which, shard):
        if which:
            rows_of = pl.ds(pl.multiple_of(core * (width // 2), width // 2), width // 2)
            return occ_all.at[pl.ds(shard * per_shard, per_shard), rows_of]
        return virt_all.at[pl.ds(pl.multiple_of(shard * rows + core * part, part), part)]

    def g_copy(j, which):
        if which:
            rows_of = pl.ds(pl.multiple_of(core * (width // 2), width // 2), width // 2)
            src = occ.at[:, rows_of]
        else:
            src = virt.at[pl.ds(pl.multiple_of(core * part, part), part)]
        return pltpu.make_async_remote_copy(
            src_ref=src,
            dst_ref=halves(which, aux),
            send_sem=g_send.at[which, j - 1],
            recv_sem=g_recv.at[which, j - 1],
            device_id={"aux": other(j)},
            device_id_type=MESH,
        )

    def s_copy(j, which):
        place = halves(which, lax.rem(aux + groups - j, groups))
        return pltpu.make_async_remote_copy(
            src_ref=place,
            dst_ref=place,
            send_sem=s_send.at[which, j - 1],
            recv_sem=s_recv.at[which, j - 1],
            device_id={"occ": sibling},
            device_id_type=MESH,
        )

    def f_copy(j):
        to = away(j)
        return pltpu.make_async_remote_copy(
            src_ref=fold.at[to],
            dst_ref=out.at[pl.ds(me * own, own)],
            send_sem=f_send.at[j - 1],
            recv_sem=f_recv.at[j - 1],
            device_id={"occ": to},
            device_id_type=MESH,
        )

    def each(action, first=1, last=None):
        def step(j, carry):
            action(j)
            return carry

        lax.fori_loop(first, peers if last is None else last, step, 0)

    for which in range(2):
        for j in range(1, groups):
            g_copy(j, which).start()
    each(lambda j: x_copy(j).start())

    for which in range(2):
        for j in range(1, groups):
            g_copy(j, which).wait_recv()
            s_copy(j, which).start()
    for copy in keep:
        copy.wait()
    for which in range(2):
        for j in range(1, groups):
            s_copy(j, which).wait_recv()
    each(lambda j: x_copy(j).wait_recv())

    for p in range(own):
        def project(g, carry):
            x = moved[:, p]
            if inner % 16:
                x = x.astype(jnp.float32)
            x = x.reshape(peers * inner, x.shape[-1]).astype(jnp.bfloat16)
            v = virt_all[pl.ds(pl.multiple_of(g * rows, rows), rows), :]
            h = lax.dot_general(
                x, v, (((1,), (1,)), ((), ())), preferred_element_type=jnp.float32
            ).astype(jnp.bfloat16)
            for t in range(per_shard):
                half[g * per_shard + t] = h[:, t * width : (t + 1) * width]
            return carry

        lax.fori_loop(0, groups, project, 0)

        def block(r, c):
            return (
                jnp.dot(occ_all[r], half[c], preferred_element_type=jnp.float32)
                .astype(jnp.bfloat16)
                .astype(jnp.float32)
            )

        def make(j):
            to = away(j)
            for s in range(MAXP):
                r = row_blocks[to * MAXP + s]
                c = col_blocks[to * MAXP + s]
                both = block(r, c) + block(c, r).T
                fold[to, p, s] = both.astype(jnp.bfloat16)

        if p < own - 1:
            each(make, 0)

    def finish(j):
        make(j)
        f_copy(j).start()

    each(finish)
    make(0)
    mine = pltpu.make_async_copy(fold.at[me], out.at[pl.ds(me * own, own)], local.at[3])
    mine.start()

    for which in range(2):
        for j in range(1, groups):
            g_copy(j, which).wait_send()
            s_copy(j, which).wait_send()
    each(lambda j: x_copy(j).wait_send())
    each(lambda j: f_copy(j).wait_recv())
    each(lambda j: f_copy(j).wait_send())
    mine.wait()


def per_device(groups, peers, amplitudes, virtual_orbitals, occupied_orbitals, screening, pair_owner, pair_weight):
    group_size, inner, virtual_count = amplitudes.shape
    rows = virtual_orbitals.shape[0]
    occupied_count = occupied_orbitals.shape[1]
    own = group_size // peers
    nblocks = screening.shape[0]
    width = pair_weight.shape[1]
    filled, row_blocks, col_blocks = slot_table(screening, pair_owner, peers * MAXP)
    kind = jnp.bfloat16
    dma = pltpu.SemaphoreType.DMA
    folded = pl.pallas_call(
        functools.partial(fused, groups, peers),
        out_shape=jax.ShapeDtypeStruct((group_size, MAXP, width, width), kind),
        in_specs=[pl.BlockSpec(memory_space=pltpu.SMEM)] * 2 + [pl.BlockSpec(memory_space=pl.ANY)] * 3,
        out_specs=pl.BlockSpec(memory_space=pl.ANY),
        scratch_shapes=[
            pltpu.VMEM((peers, own, inner, virtual_count), kind),
            pltpu.VMEM((groups * rows, virtual_count), kind),
            pltpu.VMEM((nblocks, width, occupied_count), kind),
            pltpu.VMEM((nblocks, occupied_count, width), kind),
            pltpu.VMEM((peers, own, MAXP, width, width), kind),
            dma((peers - 1,)),
            dma((peers - 1,)),
            dma((2, groups - 1)),
            dma((2, groups - 1)),
            dma((2, groups - 1)),
            dma((2, groups - 1)),
            dma((peers - 1,)),
            dma((peers - 1,)),
            dma((4,)),
        ],
        compiler_params=pltpu.CompilerParams(
            collective_id=0, has_side_effects=True, vmem_limit_bytes=40 * 1024 * 1024
        ),
    )(
        row_blocks,
        col_blocks,
        amplitudes,
        virtual_orbitals,
        occupied_orbitals.reshape(rows // width, width, occupied_count),
    )
    mine = lax.dynamic_slice_in_dim(filled, lax.axis_index("occ") * MAXP, MAXP)
    weighted = pair_weight.astype(jnp.float32)[None] * folded.astype(jnp.float32)
    return jnp.where(mine[None, :, None, None], weighted, 0.0).astype(jnp.bfloat16)


def solution(mesh):
    return jax.shard_map(
        functools.partial(per_device, mesh.shape["aux"], mesh.shape["occ"]),
        mesh=mesh,
        in_specs=(
            P("aux", "occ", None),
            P("aux", None),
            P("aux", None),
            P(),
            P(),
            P("occ", None, None),
        ),
        out_specs=P("aux", "occ", None, None),
        check_vma=False,
    )
```

time: 152 us -> 55.7 us (0.37)
  the two profiles are of different devices: /device:TPU:0 before, /device:TPU:9 now
where the time goes in v1:
time: 55.7 us; the launch traced here: 55.5 us
  Pallas kernels  49.6 us (89%)
  local copies, waits for them, and re-layouts  3.6 us (6%)
  other arithmetic  2.2 us (4%)
    pallas_call x1, Pallas kernels, per_device(): pl.pallas_call(functools.partial(fused, groups, peers), out_shape=jax.Sha...  49.6 us
    unnamed x10, local copies, waits for them, and re-layouts  3.36 us

profile of v1, /device:TPU:9, one launch (start us, length us, event | category | flops | bytes accessed | tf_op | source)
XLA Modules:
  0.0 55.5 jit_solution(3761459869470710497)
XLA Ops:
  0.0 0.0 copy-start.4
  0.0 0.7 %broadcast_compare_fusion = pred[12,12]{1,0:T(8,128)(4,1)S(1)} fusion(s32[12,12]{1,0:T(8,128)} %param.9), kind=kLoop, calls=%fused_computation.7 | loop fusion | flops 144 | bytes 720 | tf_op jit(solution)/shard_map/eq | solution.py:20
  0.7 0.1 eq.50
  0.8 0.0 copy-done.4
  0.8 0.1 reshape.51
  0.9 0.2 convert_reduce_fusion
  1.1 0.1 select_reduce_fusion
  1.3 0.0 copy-start
  1.3 1.2 %copy-done = bf16[8,64,1024]{2,1,0:T(8,128)(2,1)S(1)} copy-done((bf16[8,64,1024]{2,1,0:T(8,128)(2,1)S(1)}, bf16[8,64,1024]{2,1,0:T(8,128)(2,1)}, u32[]{:S(2)}) %copy-start) | copy-done | bytes 1048600
  2.5 0.0 copy-start.1
  2.5 1.1 %copy-done.1 = bf16[384,1024]{1,0:T(8,128)(2,1)S(1)} copy-done((bf16[384,1024]{1,0:T(8,128)(2,1)S(1)}, bf16[384,1024]{1,0:T(8,128)(2,1)}, u32[]{:S(2)}) %copy-start.1) | copy-done | bytes 786456
  3.6 0.0 copy-start.2
  3.6 1.0 %copy-done.2 = bf16[384,512]{1,0:T(8,128)(2,1)S(1)} copy-done((bf16[384,512]{1,0:T(8,128)(2,1)S(1)}, bf16[384,512]{1,0:T(8,128)(2,1)}, u32[]{:S(2)}) %copy-start.2) | copy-done | bytes 393240
  4.6 0.0 copy-start.3
  4.6 49.6 %shard_map.64 = bf16[8,2,128,128]{3,2,1,0:T(8,128)(2,1)S(1)} custom-call(s32[16]{0:T(128)S(1)} %get-tuple-element.6.row_blocks, s32[16]{0:T(128)S(1)} %get-tuple-element.5.col_blocks, bf16[8,64,1024]{2,1,0:T(8,128)(2,1)S(1)} %copy-done, bf16[384,1024]{1,0:T(8,128)(2,1)S(1)} %copy-done.1, bf16[3,128,512]{2,1,0:T(8,128)(2,1)S(1)} %bitcast.1), custom_call_target="tpu_custom_call" | custom-call | tf_op jit(solution)/shard_map/pallas_call | solution.py:217
  54.3 0.1 fusion.1
  54.4 0.1 dynamic_slice.3
  54.4 0.0 copy-done.3
  54.5 1.0 %select_convert_fusion = bf16[8,2,128,128]{3,2,1,0:T(8,128)(2,1)} fusion(bf16[8,2,128,128]{3,2,1,0:T(8,128)(2,1)S(1)} %shard_map.64, f32[2,128,128]{2,1,0:T(8,128)S(1)} %convert_element_type.13, pred[2]{0:T(512)(128)(4,1)S(1)} %dynamic_slice.3), kind=kLoop, calls=%fused_computation | loop fusion | flops 1048576 | bytes 1179650 | tf_op jit(solution)/shard_map/convert_element_type | solution.py:250
  (4 shorter events, 0.1 us)
Async XLA Ops:
  0.0 0.8 %copy-start.4 = (s32[12,12]{1,0:T(8,128)S(1)}, s32[12,12]{1,0:T(8,128)}, u32[]{:S(2)}) copy-start(s32[12,12]{1,0:T(8,128)} %param.10) | copy-start | bytes 1732
  1.3 1.2 %copy-start = (bf16[8,64,1024]{2,1,0:T(8,128)(2,1)S(1)}, bf16[8,64,1024]{2,1,0:T(8,128)(2,1)}, u32[]{:S(2)}) copy-start(bf16[8,64,1024]{2,1,0:T(8,128)(2,1)} %amp.1) | copy-start | bytes 3145732
  2.5 1.1 %copy-start.1 = (bf16[384,1024]{1,0:T(8,128)(2,1)S(1)}, bf16[384,1024]{1,0:T(8,128)(2,1)}, u32[]{:S(2)}) copy-start(bf16[384,1024]{1,0:T(8,128)(2,1)} %virt.1) | copy-start | bytes 2359300
  3.6 1.0 %copy-start.2 = (bf16[384,512]{1,0:T(8,128)(2,1)S(1)}, bf16[384,512]{1,0:T(8,128)(2,1)}, u32[]{:S(2)}) copy-start(bf16[384,512]{1,0:T(8,128)(2,1)} %param.8) | copy-start | bytes 1179652
  4.6 49.8 %copy-start.3 = (bf16[2,128,128]{2,1,0:T(8,128)(2,1)S(1)}, bf16[2,128,128]{2,1,0:T(8,128)(2,1)}, u32[]{:S(2)}) copy-start(bf16[2,128,128]{2,1,0:T(8,128)(2,1)} %param.11) | copy-start | bytes 196612

commit v2 on v1

--- a/solution.py
+++ b/solution.py
@@ -36,7 +36,7 @@
     groups, peers,
     row_blocks, col_blocks, amp, virt, occ, out,
     moved, virt_all, occ_all, half, fold,
-    x_send, x_recv, g_send, g_recv, s_send, s_recv, f_send, f_recv, local,
+    x_send, x_recv, n_send, n_recv, d_send, d_recv, s_send, s_recv, f_send, f_recv, local,
 ):
     aux = lax.axis_index("aux")
     me = lax.axis_index("occ")
@@ -45,15 +45,16 @@
     own = moved.shape[1]
     inner = moved.shape[2]
     rows = virt.shape[0]
-    part = rows // 2
-    width = half.shape[2]
+    half_group = peers // 2
+    width = half.shape[3]
     per_shard = rows // width
 
     def away(j):
         return lax.rem(me + j, peers)
 
-    def other(j):
-        return lax.rem(aux + j, groups)
+    beside = aux + 1 - 2 * lax.rem(aux, 2)
+    across = lax.rem(aux + 2, groups)
+    corner = lax.rem(beside + 2, groups)
 
     barrier = pltpu.get_barrier_semaphore()
 
@@ -62,8 +63,8 @@
         return carry
 
     lax.fori_loop(1, peers, greet, 0)
-    for j in range(1, groups):
-        pl.semaphore_signal(barrier, inc=1, device_id={"aux": other(j)}, device_id_type=MESH)
+    for near in (beside, across):
+        pl.semaphore_signal(barrier, inc=1, device_id={"aux": near}, device_id_type=MESH)
 
     keep = [
         pltpu.make_async_copy(virt, virt_all.at[pl.ds(pl.multiple_of(aux * rows, rows), rows)], local.at[0]),
@@ -72,7 +73,7 @@
     ]
     for copy in keep:
         copy.start()
-    pl.semaphore_wait(barrier, peers - 1 + groups - 1)
+    pl.semaphore_wait(barrier, peers + 1)
 
     def x_copy(j):
         to = away(j)
@@ -85,34 +86,49 @@
             device_id_type=MESH,
         )
 
-    def halves(which, shard):
+    def piece(which, shard, first, count):
         if which:
-            rows_of = pl.ds(pl.multiple_of(core * (width // 2), width // 2), width // 2)
+            quarter = width // 4
+            rows_of = pl.ds(pl.multiple_of(first * quarter, quarter), count * quarter)
             return occ_all.at[pl.ds(shard * per_shard, per_shard), rows_of]
-        return virt_all.at[pl.ds(pl.multiple_of(shard * rows + core * part, part), part)]
-
-    def g_copy(j, which):
+        quarter = rows // 4
+        return virt_all.at[pl.ds(pl.multiple_of(shard * rows + first * quarter, quarter), count * quarter)]
+
+    def n_copy(which, way, q):
+        first = 2 * core + q
         if which:
-            rows_of = pl.ds(pl.multiple_of(core * (width // 2), width // 2), width // 2)
-            src = occ.at[:, rows_of]
+            quarter = width // 4
+            src = occ.at[:, pl.ds(pl.multiple_of(first * quarter, quarter), quarter)]
         else:
-            src = virt.at[pl.ds(pl.multiple_of(core * part, part), part)]
+            quarter = rows // 4
+            src = virt.at[pl.ds(pl.multiple_of(first * quarter, quarter), quarter)]
         return pltpu.make_async_remote_copy(
             src_ref=src,
-            dst_ref=halves(which, aux),
-            send_sem=g_send.at[which, j - 1],
-            recv_sem=g_recv.at[which, j - 1],
-            device_id={"aux": other(j)},
-            device_id_type=MESH,
-        )
-
-    def s_copy(j, which):
-        place = halves(which, lax.rem(aux + groups - j, groups))
+            dst_ref=piece(which, aux, first, 1),
+            send_sem=n_send.at[which, way, q],
+            recv_sem=n_recv.at[which, way, q],
+            device_id={"aux": (beside, across)[way]},
+            device_id_type=MESH,
+        )
+
+    def d_copy(which, q):
+        place = piece(which, (beside, across)[q], 2 * core + q, 1)
         return pltpu.make_async_remote_copy(
             src_ref=place,
             dst_ref=place,
-            send_sem=s_send.at[which, j - 1],
-            recv_sem=s_recv.at[which, j - 1],
+            send_sem=d_send.at[which, q],
+            recv_sem=d_recv.at[which, q],
+            device_id={"aux": (across, beside)[q]},
+            device_id_type=MESH,
+        )
+
+    def s_copy(which, j):
+        place = piece(which, (beside, across, corner)[j], 2 * core, 2)
+        return pltpu.make_async_remote_copy(
+            src_ref=place,
+            dst_ref=place,
+            send_sem=s_send.at[which, j],
+            recv_sem=s_recv.at[which, j],
             device_id={"occ": sibling},
             device_id_type=MESH,
         )
@@ -128,62 +144,90 @@
             device_id_type=MESH,
         )
 
-    def each(action, first=1, last=None):
-        def step(j, carry):
-            action(j)
+    def each(action):
+        def step(t, carry):
+            action(half_group + (t + 1) // 2 * (2 * lax.rem(t, 2) - 1))
             return carry
 
-        lax.fori_loop(first, peers if last is None else last, step, 0)
-
-    for which in range(2):
-        for j in range(1, groups):
-            g_copy(j, which).start()
+        lax.fori_loop(0, peers - 1, step, 0)
+
+    for late in range(2):
+        for which in range(2):
+            for way in range(2):
+                n_copy(which, way, (way + late) % 2).start()
     each(lambda j: x_copy(j).start())
 
     for which in range(2):
-        for j in range(1, groups):
-            g_copy(j, which).wait_recv()
-            s_copy(j, which).start()
+        for way in range(2):
+            n_copy(which, way, way).wait_recv()
+            d_copy(which, way).start()
+    for which in range(2):
+        for way in range(2):
+            n_copy(which, way, 1 - way).wait_recv()
+            s_copy(which, way).start()
+    for which in range(2):
+        for q in range(2):
+            d_copy(which, q).wait_recv()
+        s_copy(which, 2).start()
     for copy in keep:
         copy.wait()
     for which in range(2):
-        for j in range(1, groups):
-            s_copy(j, which).wait_recv()
-    each(lambda j: x_copy(j).wait_recv())
-
-    for p in range(own):
-        def project(g, carry):
-            x = moved[:, p]
+        for j in range(3):
+            s_copy(which, j).wait_recv()
+
+    base = me // half_group * half_group
+
+    def arrived(source):
+        x_copy(lax.rem(me - source + peers, peers)).wait_recv()
+
+    def project(p, start):
+        def step(g, carry):
+            x = moved[pl.ds(start, half_group), p]
             if inner % 16:
                 x = x.astype(jnp.float32)
-            x = x.reshape(peers * inner, x.shape[-1]).astype(jnp.bfloat16)
+            count = half_group * inner
+            x = x.reshape(count, x.shape[-1]).astype(jnp.bfloat16)
             v = virt_all[pl.ds(pl.multiple_of(g * rows, rows), rows), :]
             h = lax.dot_general(
                 x, v, (((1,), (1,)), ((), ())), preferred_element_type=jnp.float32
             ).astype(jnp.bfloat16)
+            place = pl.ds(pl.multiple_of(start * inner, count), count)
             for t in range(per_shard):
-                half[g * per_shard + t] = h[:, t * width : (t + 1) * width]
+                half[p, g * per_shard + t, place, :] = h[:, t * width : (t + 1) * width]
             return carry
 
-        lax.fori_loop(0, groups, project, 0)
-
-        def block(r, c):
-            return (
-                jnp.dot(occ_all[r], half[c], preferred_element_type=jnp.float32)
-                .astype(jnp.bfloat16)
-                .astype(jnp.float32)
-            )
-
-        def make(j):
-            to = away(j)
+        lax.fori_loop(0, groups, step, 0)
+
+    def near(t, carry):
+        arrived(base + lax.rem(me - base + t, half_group))
+        return carry
+
+    def far(t, carry):
+        arrived(half_group - base + t)
+        return carry
+
+    lax.fori_loop(1, half_group, near, 0)
+    for p in range(own):
+        project(p, base)
+    lax.fori_loop(0, half_group, far, 0)
+    for p in range(own):
+        project(p, half_group - base)
+
+    def block(p, r, c):
+        return (
+            jnp.dot(occ_all[r], half[p, c], preferred_element_type=jnp.float32)
+            .astype(jnp.bfloat16)
+            .astype(jnp.float32)
+        )
+
+    def make(j):
+        to = away(j)
+        for p in range(own):
             for s in range(MAXP):
                 r = row_blocks[to * MAXP + s]
                 c = col_blocks[to * MAXP + s]
-                both = block(r, c) + block(c, r).T
+                both = block(p, r, c) + block(p, c, r).T
                 fold[to, p, s] = both.astype(jnp.bfloat16)
-
-        if p < own - 1:
-            each(make, 0)
 
     def finish(j):
         make(j)
@@ -195,9 +239,12 @@
     mine.start()
 
     for which in range(2):
-        for j in range(1, groups):
-            g_copy(j, which).wait_send()
-            s_copy(j, which).wait_send()
+        for way in range(2):
+            for q in range(2):
+                n_copy(which, way, q).wait_send()
+            d_copy(which, way).wait_send()
+        for j in range(3):
+            s_copy(which, j).wait_send()
     each(lambda j: x_copy(j).wait_send())
     each(lambda j: f_copy(j).wait_recv())
     each(lambda j: f_copy(j).wait_send())
@@ -223,20 +270,22 @@
             pltpu.VMEM((peers, own, inner, virtual_count), kind),
             pltpu.VMEM((groups * rows, virtual_count), kind),
             pltpu.VMEM((nblocks, width, occupied_count), kind),
-            pltpu.VMEM((nblocks, occupied_count, width), kind),
+            pltpu.VMEM((own, nblocks, occupied_count, width), kind),
             pltpu.VMEM((peers, own, MAXP, width, width), kind),
             dma((peers - 1,)),
             dma((peers - 1,)),
-            dma((2, groups - 1)),
-            dma((2, groups - 1)),
-            dma((2, groups - 1)),
-            dma((2, groups - 1)),
+            dma((2, 2, 2)),
+            dma((2, 2, 2)),
+            dma((2, 2)),
+            dma((2, 2)),
+            dma((2, 3)),
+            dma((2, 3)),
             dma((peers - 1,)),
             dma((peers - 1,)),
             dma((4,)),
         ],
         compiler_params=pltpu.CompilerParams(
-            collective_id=0, has_side_effects=True, vmem_limit_bytes=40 * 1024 * 1024
+            collective_id=0, has_side_effects=True, vmem_limit_bytes=60 * 1024 * 1024
         ),
     )(
         row_blocks,

time: 55.7 us -> 49.2 us (0.88)
  the two profiles are of different devices: /device:TPU:9 before, /device:TPU:0 now
where the time goes in v2:
time: 49.2 us; the launch traced here: 49 us
  Pallas kernels  44.9 us (91%)
  other arithmetic  3.84 us (8%)
    pallas_call x1, Pallas kernels, per_device(): pl.pallas_call(functools.partial(fused, groups, peers), out_shape=jax.Sha...  44.9 us
    convert_element_type x1, other arithmetic, per_device(): jnp.where(mine[None, :, None, None], weighted, 0.0).astype(jnp.bfloat16)  2.04 us

profile of v2, /device:TPU:0, one launch (start us, length us, event | category | flops | bytes accessed | tf_op | source)
XLA Modules:
  0.0 49.0 jit_solution(4295352117514867953)
XLA Ops:
  0.0 0.0 copy-start.1
  0.0 0.7 %broadcast_compare_fusion = pred[12,12]{1,0:T(8,128)(4,1)S(1)} fusion(s32[12,12]{1,0:T(8,128)} %param.9), kind=kLoop, calls=%fused_computation.7 | loop fusion | flops 144 | bytes 720 | tf_op jit(solution)/shard_map/eq | solution.py:20
  0.7 0.1 eq.50
  0.8 0.0 copy-done.1
  0.8 0.1 reshape.51
  0.9 0.2 convert_reduce_fusion
  1.1 0.1 select_reduce_fusion
  1.3 0.6 %and_select_fusion = (s32[16]{0:T(128)}, s32[16]{0:T(128)}) fusion(s32[16]{0:T(128)S(1)} %select_reduce_fusion), kind=kLoop, calls=%fused_computation.11 | loop fusion | flops 192 | bytes 192 | tf_op jit(solution)/shard_map/jit(remainder)/select_n | solution.py:32
  1.9 0.0 copy-start
  1.9 44.9 %shard_map.64 = bf16[8,2,128,128]{3,2,1,0:T(8,128)(2,1)} custom-call(s32[16]{0:T(128)} %get-tuple-element.6.row_blocks, s32[16]{0:T(128)} %get-tuple-element.5.col_blocks, bf16[8,64,1024]{2,1,0:T(8,128)(2,1)} %amp.1, bf16[384,1024]{1,0:T(8,128)(2,1)} %virt.1, bf16[3,128,512]{2,1,0:T(8,128)(2,1)} %bitcast.1), custom_call_target="tpu_custom_call" | custom-call | tf_op jit(solution)/shard_map/pallas_call | solution.py:264
  46.7 0.1 fusion.1
  46.9 0.1 dynamic_slice.3
  46.9 0.0 copy-done
  47.0 2.0 %select_convert_fusion = bf16[8,2,128,128]{3,2,1,0:T(8,128)(2,1)} fusion(bf16[8,2,128,128]{3,2,1,0:T(8,128)(2,1)} %shard_map.64, f32[2,128,128]{2,1,0:T(8,128)S(1)} %convert_element_type.13, pred[2]{0:T(512)(128)(4,1)S(1)} %dynamic_slice.3), kind=kLoop, calls=%fused_computation | loop fusion | flops 1048576 | bytes 1179650 | tf_op jit(solution)/shard_map/convert_element_type | solution.py:299
  (3 shorter events, 0.0 us)
Async XLA Ops:
  0.0 0.8 %copy-start.1 = (s32[12,12]{1,0:T(8,128)S(1)}, s32[12,12]{1,0:T(8,128)}, u32[]{:S(2)}) copy-start(s32[12,12]{1,0:T(8,128)} %param.10) | copy-start | bytes 1732
  1.9 45.1 %copy-start = (bf16[2,128,128]{2,1,0:T(8,128)(2,1)S(1)}, bf16[2,128,128]{2,1,0:T(8,128)(2,1)}, u32[]{:S(2)}) copy-start(bf16[2,128,128]{2,1,0:T(8,128)(2,1)} %param.11) | copy-start | bytes 196612

commit v3 on v2

--- a/solution.py
+++ b/solution.py
@@ -151,29 +151,38 @@
 
         lax.fori_loop(0, peers - 1, step, 0)
 
-    for late in range(2):
-        for which in range(2):
+    def spread(which):
+        for late in range(2):
             for way in range(2):
                 n_copy(which, way, (way + late) % 2).start()
-    each(lambda j: x_copy(j).start())
-
-    for which in range(2):
+
+    def pass_on(which):
         for way in range(2):
             n_copy(which, way, way).wait_recv()
             d_copy(which, way).start()
-    for which in range(2):
+
+    def share_sides(which):
         for way in range(2):
             n_copy(which, way, 1 - way).wait_recv()
             s_copy(which, way).start()
-    for which in range(2):
+
+    def share_corner(which):
         for q in range(2):
             d_copy(which, q).wait_recv()
         s_copy(which, 2).start()
+
+    spread(0)
+    each(lambda j: x_copy(j).start())
+    pass_on(0)
+    spread(1)
+    share_sides(0)
+    share_corner(0)
+    pass_on(1)
+    share_sides(1)
     for copy in keep:
         copy.wait()
-    for which in range(2):
-        for j in range(3):
-            s_copy(which, j).wait_recv()
+    for j in range(3):
+        s_copy(0, j).wait_recv()
 
     base = me // half_group * half_group
 
@@ -209,9 +218,13 @@
     lax.fori_loop(1, half_group, near, 0)
     for p in range(own):
         project(p, base)
+    share_corner(1)
     lax.fori_loop(0, half_group, far, 0)
     for p in range(own):
         project(p, half_group - base)
+
+    for j in range(3):
+        s_copy(1, j).wait_recv()
 
     def block(p, r, c):
         return (

time: 49.2 us -> 45.9 us (0.933)
  Pallas kernels: 44.9 us -> 41.4 us
    pallas_call x1, Pallas kernels: 44.9 us -> 41.4 us  [per_device(): pl.pallas_call(functools.partial(fused, groups, peers), out_shape=jax.Sha...]
where the time goes in v3:
time: 45.9 us; the launch traced here: 45.5 us
  Pallas kernels  41.4 us (90%)
  other arithmetic  3.84 us (8%)
    pallas_call x1, Pallas kernels, per_device(): pl.pallas_call(functools.partial(fused, groups, peers), out_shape=jax.Sha...  41.4 us
    convert_element_type x1, other arithmetic, per_device(): jnp.where(mine[None, :, None, None], weighted, 0.0).astype(jnp.bfloat16)  2.04 us

profile of v3, /device:TPU:0, one launch (start us, length us, event | category | flops | bytes accessed | tf_op | source)
XLA Modules:
  0.0 45.5 jit_solution(15392036132022516484)
XLA Ops:
  0.0 0.0 copy-start.1
  0.0 0.7 %broadcast_compare_fusion = pred[12,12]{1,0:T(8,128)(4,1)S(1)} fusion(s32[12,12]{1,0:T(8,128)} %param.9), kind=kLoop, calls=%fused_computation.7 | loop fusion | flops 144 | bytes 720 | tf_op jit(solution)/shard_map/eq | solution.py:20
  0.7 0.1 eq.50
  0.8 0.0 copy-done.1
  0.8 0.1 reshape.51
  0.9 0.2 convert_reduce_fusion
  1.1 0.1 select_reduce_fusion
  1.3 0.6 %and_select_fusion = (s32[16]{0:T(128)}, s32[16]{0:T(128)}) fusion(s32[16]{0:T(128)S(1)} %select_reduce_fusion), kind=kLoop, calls=%fused_computation.11 | loop fusion | flops 192 | bytes 192 | tf_op jit(solution)/shard_map/jit(remainder)/select_n | solution.py:32
  1.9 0.0 copy-start
  1.9 41.4 %shard_map.64 = bf16[8,2,128,128]{3,2,1,0:T(8,128)(2,1)} custom-call(s32[16]{0:T(128)} %get-tuple-element.6.row_blocks, s32[16]{0:T(128)} %get-tuple-element.5.col_blocks, bf16[8,64,1024]{2,1,0:T(8,128)(2,1)} %amp.1, bf16[384,1024]{1,0:T(8,128)(2,1)} %virt.1, bf16[3,128,512]{2,1,0:T(8,128)(2,1)} %bitcast.1), custom_call_target="tpu_custom_call" | custom-call | tf_op jit(solution)/shard_map/pallas_call | solution.py:277
  43.3 0.1 fusion.1
  43.4 0.1 dynamic_slice.3
  43.5 0.0 copy-done
  43.5 2.0 %select_convert_fusion = bf16[8,2,128,128]{3,2,1,0:T(8,128)(2,1)} fusion(bf16[8,2,128,128]{3,2,1,0:T(8,128)(2,1)} %shard_map.64, f32[2,128,128]{2,1,0:T(8,128)S(1)} %convert_element_type.13, pred[2]{0:T(512)(128)(4,1)S(1)} %dynamic_slice.3), kind=kLoop, calls=%fused_computation | loop fusion | flops 1048576 | bytes 1179650 | tf_op jit(solution)/shard_map/convert_element_type | solution.py:312
  (3 shorter events, 0.0 us)
Async XLA Ops:
  0.0 0.8 %copy-start.1 = (s32[12,12]{1,0:T(8,128)S(1)}, s32[12,12]{1,0:T(8,128)}, u32[]{:S(2)}) copy-start(s32[12,12]{1,0:T(8,128)} %param.10) | copy-start | bytes 1732
  1.9 41.6 %copy-start = (bf16[2,128,128]{2,1,0:T(8,128)(2,1)S(1)}, bf16[2,128,128]{2,1,0:T(8,128)(2,1)}, u32[]{:S(2)}) copy-start(bf16[2,128,128]{2,1,0:T(8,128)(2,1)} %param.11) | copy-start | bytes 196612

commit v4 on v3

--- a/solution.py
+++ b/solution.py
@@ -11,31 +11,32 @@
 MESH = pl.DeviceIdType.MESH
 
 
-def slot_table(screening, pair_owner, slots):
-    nblocks = screening.shape[0]
-    count = nblocks * nblocks
-    block_ids = jnp.arange(count, dtype=jnp.int32)
-    first = block_ids // nblocks
-    second = block_ids % nblocks
-    keep_flag = (screening.reshape(count) == 1) & (first <= second)
-    owner_flat = pair_owner.reshape(count)
-    earlier = (
-        (owner_flat[:, None] == owner_flat[None, :])
-        & keep_flag[None, :]
-        & (block_ids[None, :] < block_ids[:, None])
-    )
-    ranks = jnp.sum(earlier.astype(jnp.int32), axis=1)
-    target = jnp.where(keep_flag, owner_flat * MAXP + ranks, -1)
-    matches = target[None, :] == jnp.arange(slots, dtype=jnp.int32)[:, None]
-    filled = jnp.any(matches, axis=1)
-    chosen = jnp.sum(jnp.where(matches, block_ids[None, :], 0), axis=1)
-    return filled, chosen // nblocks, chosen % nblocks
+def slot_table(screening, pair_owner, nblocks, lanes):
+    lane = lax.broadcasted_iota(jnp.int32, (1, lanes), 1)
+    owner, rank = lane // MAXP, lane % MAXP
+
+    def row(r, carry):
+        def column(c, carry):
+            rows, columns, filled, count = carry
+            kept = (owner == pair_owner[r, c]) & (jnp.full_like(lane, screening[r, c]) == 1)
+            here = kept & (rank == count)
+            return (
+                jnp.where(here, r, rows),
+                jnp.where(here, c, columns),
+                jnp.where(here, 1, filled),
+                jnp.where(kept, count + 1, count),
+            )
+
+        return lax.fori_loop(r, nblocks, column, carry)
+
+    none = jnp.zeros_like(lane)
+    return lax.fori_loop(0, nblocks, row, (none,) * 4)[:3]
 
 
 def fused(
     groups, peers,
-    row_blocks, col_blocks, amp, virt, occ, out,
-    moved, virt_all, occ_all, half, fold,
+    screening, pair_owner, amp, virt, occ, out,
+    moved, virt_all, occ_all, half, fold, lines, table,
     x_send, x_recv, n_send, n_recv, d_send, d_recv, s_send, s_recv, f_send, f_recv, local,
 ):
     aux = lax.axis_index("aux")
@@ -173,6 +174,12 @@
 
     spread(0)
     each(lambda j: x_copy(j).start())
+    for line, values in enumerate(slot_table(screening, pair_owner, half.shape[1], lines.shape[1])):
+        lines[line : line + 1, :] = values
+    for line in range(3, lines.shape[0]):
+        lines[line : line + 1, :] = jnp.zeros_like(values)
+    to_scalars = pltpu.make_async_copy(lines, table, local.at[4])
+    to_scalars.start()
     pass_on(0)
     spread(1)
     share_sides(0)
@@ -225,6 +232,7 @@
 
     for j in range(3):
         s_copy(1, j).wait_recv()
+    to_scalars.wait()
 
     def block(p, r, c):
         return (
@@ -237,9 +245,10 @@
         to = away(j)
         for p in range(own):
             for s in range(MAXP):
-                r = row_blocks[to * MAXP + s]
-                c = col_blocks[to * MAXP + s]
-                both = block(p, r, c) + block(p, c, r).T
+                r = table[0, to * MAXP + s]
+                c = table[1, to * MAXP + s]
+                filled = table[2, to * MAXP + s].astype(jnp.float32)
+                both = (block(p, r, c) + block(p, c, r).T) * filled
                 fold[to, p, s] = both.astype(jnp.bfloat16)
 
     def finish(j):
@@ -271,7 +280,7 @@
     own = group_size // peers
     nblocks = screening.shape[0]
     width = pair_weight.shape[1]
-    filled, row_blocks, col_blocks = slot_table(screening, pair_owner, peers * MAXP)
+    lanes = -(-peers * MAXP // 128) * 128
     kind = jnp.bfloat16
     dma = pltpu.SemaphoreType.DMA
     folded = pl.pallas_call(
@@ -285,6 +294,8 @@
             pltpu.VMEM((nblocks, width, occupied_count), kind),
             pltpu.VMEM((own, nblocks, occupied_count, width), kind),
             pltpu.VMEM((peers, own, MAXP, width, width), kind),
+            pltpu.VMEM((8, lanes), jnp.int32),
+            pltpu.SMEM((8, lanes), jnp.int32),
             dma((peers - 1,)),
             dma((peers - 1,)),
             dma((2, 2, 2)),
@@ -295,21 +306,20 @@
             dma((2, 3)),
             dma((peers - 1,)),
             dma((peers - 1,)),
-            dma((4,)),
+            dma((5,)),
         ],
         compiler_params=pltpu.CompilerParams(
             collective_id=0, has_side_effects=True, vmem_limit_bytes=60 * 1024 * 1024
         ),
     )(
-        row_blocks,
-        col_blocks,
+        screening,
+        pair_owner,
         amplitudes,
         virtual_orbitals,
         occupied_orbitals.reshape(rows // width, width, occupied_count),
     )
-    mine = lax.dynamic_slice_in_dim(filled, lax.axis_index("occ") * MAXP, MAXP)
-    weighted = pair_weight.astype(jnp.float32)[None] * folded.astype(jnp.float32)
-    return jnp.where(mine[None, :, None, None], weighted, 0.0).astype(jnp.bfloat16)
+    weights = pair_weight.astype(jnp.float32)[None]
+    return (weights * folded.astype(jnp.float32)).astype(jnp.bfloat16)
 
 
 def solution(mesh):

time: 45.9 us -> 44.8 us (0.976)
  other arithmetic: 3.84 us -> 2.83 us
    convert_element_type x2, other arithmetic: 2.05 us -> 2.83 us  [the longest x1 1.98 us: per_device(): return (weights * folded.astype(jnp.float32)).astype(jnp.bfloat16)]
    eq x1 -> x0, other arithmetic: 0.71 us -> none  [slot_table(): keep_flag = (screening.reshape(count) == 1) & (first <= second)]
    select_n x2 -> x0, other arithmetic: 0.64 us -> none  [the longest x1 0.62 us: slot_table(): return (filled, chosen // nblocks, chosen % nblocks)]
where the time goes in v4:
time: 44.8 us; the launch traced here: 44.4 us
  Pallas kernels  41.6 us (93%)
  other arithmetic  2.83 us (6%)
    pallas_call x1, Pallas kernels, per_device(): pl.pallas_call(functools.partial(fused, groups, peers), out_shape=jax.Sha...  41.6 us
    convert_element_type x1, other arithmetic, per_device(): return (weights * folded.astype(jnp.float32)).astype(jnp.bfloat16)  1.98 us

profile of v4, /device:TPU:0, one launch (start us, length us, event | category | flops | bytes accessed | tf_op | source)
XLA Modules:
  0.0 44.4 jit_solution(17000990419924732915)
XLA Ops:
  0.0 0.8 %convert_element_type.9 = f32[2,128,128]{2,1,0:T(8,128)S(1)} convert(bf16[2,128,128]{2,1,0:T(8,128)(2,1)} %param.11) | non-fusion elementwise | flops 32768 | bytes 196608 | tf_op jit(solution)/shard_map/convert_element_type | solution.py:321
  0.9 41.6 %shard_map.64 = bf16[8,2,128,128]{3,2,1,0:T(8,128)(2,1)} custom-call(s32[12,12]{1,0:T(8,128)} %screening.1, s32[12,12]{1,0:T(8,128)} %pair_owner.1, bf16[8,64,1024]{2,1,0:T(8,128)(2,1)} %amp.1, bf16[384,1024]{1,0:T(8,128)(2,1)} %virt.1, bf16[3,128,512]{2,1,0:T(8,128)(2,1)} %bitcast.1), custom_call_target="tpu_custom_call" | custom-call | tf_op jit(solution)/shard_map/pallas_call | solution.py:286
  42.4 2.0 %multiply_convert_fusion = bf16[8,2,128,128]{3,2,1,0:T(8,128)(2,1)} fusion(bf16[8,2,128,128]{3,2,1,0:T(8,128)(2,1)} %shard_map.64, f32[2,128,128]{2,1,0:T(8,128)S(1)} %convert_element_type.9), kind=kLoop, calls=%fused_computation | loop fusion | flops 786432 | bytes 1179648 | tf_op jit(solution)/shard_map/convert_element_type | solution.py:322

commit v5 on v4

--- a/solution.py
+++ b/solution.py
@@ -74,6 +74,12 @@
     ]
     for copy in keep:
         copy.start()
+    for line, values in enumerate(slot_table(screening, pair_owner, half.shape[1], lines.shape[1])):
+        lines[line : line + 1, :] = values
+    for line in range(3, lines.shape[0]):
+        lines[line : line + 1, :] = jnp.zeros_like(values)
+    to_scalars = pltpu.make_async_copy(lines, table, local.at[4])
+    to_scalars.start()
     pl.semaphore_wait(barrier, peers + 1)
 
     def x_copy(j):
@@ -174,12 +180,6 @@
 
     spread(0)
     each(lambda j: x_copy(j).start())
-    for line, values in enumerate(slot_table(screening, pair_owner, half.shape[1], lines.shape[1])):
-        lines[line : line + 1, :] = values
-    for line in range(3, lines.shape[0]):
-        lines[line : line + 1, :] = jnp.zeros_like(values)
-    to_scalars = pltpu.make_async_copy(lines, table, local.at[4])
-    to_scalars.start()
     pass_on(0)
     spread(1)
     share_sides(0)

time: 44.8 us -> 44.9 us (level)
  no operation moved by 1% of the time
where the time goes in v5:
time: 44.9 us; the launch traced here: 44.6 us
  Pallas kernels  41.8 us (93%)
  other arithmetic  2.83 us (6%)
    pallas_call x1, Pallas kernels, per_device(): pl.pallas_call(functools.partial(fused, groups, peers), out_shape=jax.Sha...  41.8 us
    convert_element_type x1, other arithmetic, per_device(): return (weights * folded.astype(jnp.float32)).astype(jnp.bfloat16)  1.98 us

profile of v5, /device:TPU:0, one launch (start us, length us, event | category | flops | bytes accessed | tf_op | source)
XLA Modules:
  0.0 44.6 jit_solution(7472955275045107083)
XLA Ops:
  0.0 0.8 %convert_element_type.9 = f32[2,128,128]{2,1,0:T(8,128)S(1)} convert(bf16[2,128,128]{2,1,0:T(8,128)(2,1)} %param.11) | non-fusion elementwise | flops 32768 | bytes 196608 | tf_op jit(solution)/shard_map/convert_element_type | solution.py:321
  0.9 41.8 %shard_map.64 = bf16[8,2,128,128]{3,2,1,0:T(8,128)(2,1)} custom-call(s32[12,12]{1,0:T(8,128)} %screening.1, s32[12,12]{1,0:T(8,128)} %pair_owner.1, bf16[8,64,1024]{2,1,0:T(8,128)(2,1)} %amp.1, bf16[384,1024]{1,0:T(8,128)(2,1)} %virt.1, bf16[3,128,512]{2,1,0:T(8,128)(2,1)} %bitcast.1), custom_call_target="tpu_custom_call" | custom-call | tf_op jit(solution)/shard_map/pallas_call | solution.py:286
  42.7 2.0 %multiply_convert_fusion = bf16[8,2,128,128]{3,2,1,0:T(8,128)(2,1)} fusion(bf16[8,2,128,128]{3,2,1,0:T(8,128)(2,1)} %shard_map.64, f32[2,128,128]{2,1,0:T(8,128)S(1)} %convert_element_type.9), kind=kLoop, calls=%fused_computation | loop fusion | flops 786432 | bytes 1179648 | tf_op jit(solution)/shard_map/convert_element_type | solution.py:322
